TPU v7x, 32 devices: a whole 2x2x4 slice. The times are simulated.
32 devices in a mesh: ctx: 4 (over y, x), tp: 8 (over z, core).
Axes of the slice: x: 2, y: 2, z: 4, core: 2. Of those that a mesh axis runs over, the one named last changes fastest.
Arguments:
- normed_rows: bfloat16 [3072, 4096], P(('ctx', 'tp')), may hold values from -6 to 6
- out_grad: bfloat16 [3072, 4096], P(('ctx', 'tp')), may hold values from -6 to 6
- inner_weight: bfloat16 [2, 4096, 2048], P(None, None, 'tp'), may hold values from -0.09375 to 0.09375
- state_weight: bfloat16 [4096, 256], replicated, may hold values from -0.09375 to 0.09375
- step_weight: bfloat16 [4096, 16], P(None, 'tp'), may hold values from -0.09375 to 0.09375
- conv_inner: float32 [4, 2048], P(None, 'tp'), may hold values from -3 to 3
- conv_state: float32 [4, 256], replicated, may hold values from -3 to 3
- step_bias: float32 [16], P('tp'), may hold values from -4 to -1
- decay_log: float32 [16], P('tp')
- norm_gain: float32 [2048], P('tp'), may hold values from 0.1 to 1.9
- out_weight: bfloat16 [2048, 4096], P('tp'), may hold values from -0.125 to 0.125
Outputs:
- input_grad: bfloat16 [3072, 4096], P(('ctx', 'tp'))
All inputs are finite; a program needn't handle non-finite values.
Results may differ from a plain program's by a relative error of at most 0.0095.
Values may be sent and summed in bfloat16 or wider, within the bound.
No kernel may reach another device: no remote copies, remote signals or barrier semaphores. Data moves between devices by JAX's collectives and lax.ppermute only.
A program may use at most 128 MiB of HBM per device.

v0:
```python
from functools import partial

import jax
import jax.numpy as jnp
from jax import lax
from jax.sharding import PartitionSpec as P

HEAD_DIM = 128
STATE = 128
CONV = 4


EPSILON = 1e-05
EXACT = lax.Precision.HIGHEST


def shifted(value, axis, by):
    length = lax.axis_size(axis)
    pairs = [(i, i + by) for i in range(length) if 0 <= i + by < length]
    return lax.ppermute(value, axis, pairs)


def prefix(value, axis, combine, identity, reverse):
    length, mine = (lax.axis_size(axis), lax.axis_index(axis))
    everything = jax.tree.map(lambda part: lax.all_gather(part, axis), value)
    start = jax.tree.map(
        lambda part, zero: jnp.broadcast_to(jnp.asarray(zero, part.dtype), part.shape),
        value,
        identity,
    )

    def turn(k, before):
        at = length - 1 - k if reverse else k
        reached = at > mine if reverse else at < mine
        new = combine(before, jax.tree.map(lambda part: part[at], everything))
        return jax.tree.map(lambda a, b: jnp.where(reached, a, b), new, before)

    return lax.fori_loop(0, length, turn, start)


def decay_table(log_decay):
    running = jnp.cumsum(log_decay, axis=0)
    length = log_decay.shape[0]
    causal = (
        lax.broadcasted_iota(jnp.int32, (length, length), 0)
        >= lax.broadcasted_iota(jnp.int32, (length, length), 1)
    ).astype(jnp.float32)
    spread_log = running.T[:, :, None] - running.T[:, None, :]
    return (running, jnp.exp(jnp.minimum(spread_log, 0.0)) * causal)


def within_shard(inner_act, step_size, log_decay, b_rows, c_rows, entering):
    running, decays = decay_table(log_decay)
    scores = jnp.dot(c_rows, b_rows.T, precision=EXACT)
    weights = decays * scores[None] * step_size.T[:, None, :]
    local_part = jnp.einsum("hts,shp->thp", weights, inner_act, precision=EXACT)
    carried = (
        jnp.einsum("tn,hpn->thp", c_rows, entering, precision=EXACT) * jnp.exp(running)[:, :, None]
    )
    return local_part + carried


def leaving_state(inner_act, step_size, log_decay, b_rows, entering):
    running = jnp.cumsum(log_decay, axis=0)
    weights = jnp.exp(running[-1][None, :] - running) * step_size
    own_state = jnp.einsum("th,thp,tn->hpn", weights, inner_act, b_rows, precision=EXACT)
    return jnp.exp(running[-1])[:, None, None] * entering + own_state


def conv_pieces(extended, step_raw, kernel, step_bias, decay_rates, inner_width):
    length = step_raw.shape[0]
    blended = jnp.zeros((length, extended.shape[1]), jnp.float32)
    for offset in range(kernel.shape[0]):
        blended = blended + kernel[offset] * extended[offset : offset + length]
    active = jax.nn.silu(blended)
    state_half = (extended.shape[1] - inner_width) // 2
    inner_act = active[:, :inner_width].reshape(length, -1, HEAD_DIM)
    b_rows = active[:, inner_width : inner_width + state_half]
    c_rows = active[:, inner_width + state_half :]
    step_size = jax.nn.softplus(step_raw + step_bias)
    return (inner_act, b_rows, c_rows, step_size, -step_size * decay_rates)


def forward_combine(earlier, later):
    return (earlier[0] * later[0], later[0][:, None, None] * earlier[1] + later[1])


def backward_combine(earlier, later):
    return (earlier[0] * later[0], later[1] + later[0][:, None, None] * earlier[1])


def body(
    normed_rows,
    out_grad,
    inner_weight,
    state_weight,
    step_weight,
    conv_inner,
    conv_state,
    step_bias,
    decay_log,
    norm_gain,
    out_weight,
):
    inner_width = inner_weight.shape[2]
    state_width = state_weight.shape[1]
    head_count = step_bias.shape[0]
    rows_all, grads_all = (
        lax.all_gather(normed_rows, "tp", axis=0, tiled=True),
        lax.all_gather(out_grad, "tp", axis=0, tiled=True),
    )
    projected = jnp.concatenate(
        [
            jnp.dot(rows_all, inner_weight[0], preferred_element_type=jnp.float32),
            jnp.dot(rows_all, inner_weight[1], preferred_element_type=jnp.float32),
            jnp.dot(rows_all, state_weight, preferred_element_type=jnp.float32),
            jnp.dot(rows_all, step_weight, preferred_element_type=jnp.float32),
        ],
        axis=1,
    )
    length = projected.shape[0]
    gate_raw = projected[:, :inner_width].astype(jnp.bfloat16)
    conv_in = projected[:, inner_width : 2 * inner_width + state_width].astype(jnp.bfloat16)
    step_raw = projected[:, 2 * inner_width + state_width :].astype(jnp.bfloat16)
    tail_rows = shifted(conv_in[length - (CONV - 1) :], "ctx", 1)
    extended = jnp.concatenate([tail_rows, conv_in], axis=0).astype(jnp.float32)
    kernel = jnp.concatenate([conv_inner, conv_state], axis=1)
    decay_rates = jnp.exp(decay_log)
    pieces_fn = partial(
        conv_pieces,
        kernel=kernel,
        step_bias=step_bias,
        decay_rates=decay_rates,
        inner_width=inner_width,
    )
    pieces, pull_pieces = jax.vjp(pieces_fn, extended, step_raw.astype(jnp.float32))
    inner_act, b_rows, c_rows, step_size, log_decay = pieces
    zero_state = jnp.zeros((head_count, HEAD_DIM, STATE), jnp.float32)
    own_state = leaving_state(inner_act, step_size, log_decay, b_rows, zero_state)
    shard_decay = jnp.exp(jnp.sum(log_decay, axis=0))
    identity = (jnp.ones_like(shard_decay), jnp.zeros_like(own_state))
    entering = prefix((shard_decay, own_state), "ctx", forward_combine, identity, False)[1]
    scan_out, pull_scan = jax.vjp(
        within_shard, inner_act, step_size, log_decay, b_rows, c_rows, entering
    )
    scan_flat = scan_out.reshape(length, inner_width)
    gate_float = gate_raw.astype(jnp.float32)
    gate_act = jax.nn.silu(gate_float)
    gated_out = scan_flat * gate_act
    out_local = jnp.dot(grads_all, out_weight.T, preferred_element_type=jnp.float32)
    token_totals = lax.psum(
        (
            jnp.sum(gated_out * gated_out, axis=1),
            jnp.sum(norm_gain * out_local * gated_out, axis=1),
        ),
        "tp",
    )
    total_width = inner_width * lax.axis_size("tp")
    inverse = lax.rsqrt(token_totals[0] / total_width + EPSILON)[:, None]
    d_gated = (
        inverse * norm_gain * out_local
        - gated_out * (inverse * inverse * inverse) * (token_totals[1] / total_width)[:, None]
    )
    gate_sigmoid = jax.nn.sigmoid(gate_float)
    d_gate = d_gated * scan_flat * gate_sigmoid * (1.0 + gate_float * (1.0 - gate_sigmoid))
    d_scan = (d_gated * gate_act).reshape(length, head_count, HEAD_DIM)
    d_inner, d_step, d_decay, d_brows, d_crows, d_entering = pull_scan(d_scan)
    leaving_grad = prefix((shard_decay, d_entering), "ctx", backward_combine, identity, True)[1]
    _, pull_leave = jax.vjp(
        partial(leaving_state, entering=entering), inner_act, step_size, log_decay, b_rows
    )
    leave_grads = pull_leave(leaving_grad)
    d_extended, d_step_raw = pull_pieces(
        (
            d_inner + leave_grads[0],
            d_brows + leave_grads[3],
            d_crows,
            d_step + leave_grads[1],
            d_decay + leave_grads[2],
        )
    )
    incoming = shifted(d_extended[: CONV - 1], "ctx", -1)
    d_conv = jnp.concatenate(
        [d_extended[CONV - 1 : length], d_extended[length:] + incoming], axis=0
    )
    d_gate_half = d_gate.astype(jnp.bfloat16)
    d_inner_half = d_conv[:, :inner_width].astype(jnp.bfloat16)
    d_state = d_conv[:, inner_width:]
    d_step_half = d_step_raw.astype(jnp.bfloat16)
    state_float = state_weight.astype(jnp.float32)
    summed_term = jnp.dot(d_gate_half, inner_weight[0].T, preferred_element_type=jnp.float32)
    summed_term = summed_term + jnp.dot(
        d_inner_half, inner_weight[1].T, preferred_element_type=jnp.float32
    )
    summed_term = summed_term + jnp.dot(
        d_step_half, step_weight.T, preferred_element_type=jnp.float32
    )
    summed_term = summed_term + jnp.dot(
        d_state, state_float.T, precision=EXACT, preferred_element_type=jnp.float32
    )
    result = lax.psum_scatter(summed_term, "tp", scatter_dimension=0, tiled=True)
    return result.astype(jnp.bfloat16)


def solution(mesh):
    placed = (
        P(("ctx", "tp"), None),
        P(("ctx", "tp"), None),
        P(None, None, "tp"),
        P(),
        P(None, "tp"),
        P(None, "tp"),
        P(),
        P("tp"),
        P("tp"),
        P("tp"),
        P("tp", None),
    )
    return jax.shard_map(
        body, mesh=mesh, in_specs=placed, out_specs=P(("ctx", "tp"), None), check_vma=False
    )
```

profile of v0, /device:TPU:4, one launch (start us, length us, event | category | flops | bytes accessed | tf_op | source)
XLA Modules:
  0.0 459.0 jit_solution(6624421825671193793)
XLA Ops:
  13.8 61.2 %all-gather.6.cloned.1.call-done = bf16[768,4096]{1,0:T(8,128)(2,1)} async-done(((bf16[96,4096]{1,0:T(8,128)(2,1)}), bf16[768,4096]{1,0:T(8,128)(2,1)}) %all-gather.6.cloned.1.call-update) | async-done | bytes 6291472 | tf_op jit(solution)/shard_map/all_gather | solution.py:109
  75.0 4.5 negate_multiply_fusion
  80.5 5.1 %convolution_convert_fusion = bf16[768,256]{0,1:T(8,128)(2,1)S(1)} fusion(bf16[768,4096]{1,0:T(8,128)(2,1)} %all-gather.6.cloned.1.call-done, bf16[4096,256]{1,0:T(8,128)(2,1)S(1)} %copy-done), kind=kOutput, calls=%fused_computation.70 | convolution fusion | flops 1610809344 | bytes 8781824 | tf_op jit(solution)/shard_map/dot_general | solution.py:116
  89.5 3.4 collective-permute-start
  93.5 46.6 %all-gather.8.cloned.1.call-done = bf16[768,4096]{1,0:T(8,128)(2,1)} async-done(((bf16[96,4096]{1,0:T(8,128)(2,1)}), bf16[768,4096]{1,0:T(8,128)(2,1)}) %all-gather.8.cloned.1.call-update) | async-done | bytes 6291472 | tf_op jit(solution)/shard_map/all_gather | solution.py:110
  140.1 6.1 %fusion.133 = f32[768,256]{0,1:T(8,128)} fusion(bf16[768,4096]{1,0:T(8,128)(2,1)} %all-gather.8.cloned.1.call-done, bf16[256,4096]{1,0:T(8,128)(2,1)} %param.25), kind=kOutput, calls=%fused_computation.185 | convolution fusion | flops 1610612736 | bytes 9175040 | tf_op jit(solution)/shard_map/dot_general | solution.py:150
  146.2 9.5 %all-reduce.9 = f32[8]{0:T(128)S(1)} all-reduce(f32[8]{0:T(128)S(1)} %exponential_dynamic-update-slice_fusion), channel_id=2, replica_groups=mesh['ctx'=4,'tp'=8] {'ctx'}, use_global_device_ids=true, to_apply=%add.9 | all-reduce | flops 8 | bytes 64
  159.0 3.5 fusion.97
  163.3 11.3 %all-gather.1 = f32[8,128,128]{2,1,0:T(8,128)} all-gather(f32[2,128,128]{2,1,0:T(8,128)S(1)} %convolution_add_fusion.2), channel_id=3, replica_groups=mesh['ctx'=4,'tp'=8] {'ctx'}, dimensions={0}, use_global_device_ids=true | all-gather | bytes 655360 | tf_op jit(solution)/shard_map/all_gather | solution.py:25
  174.6 4.1 while.30
  181.4 8.3 %fusion.56 = f32[768,2,128]{0,2,1:T(8,128)S(1)} fusion(f32[768,2,128]{0,2,1:T(8,128)S(1)} %bitcast.194, f32[2,768]{1,0:T(2,128)S(1)} %get-tuple-element.304, f32[768,768]{1,0:T(8,128)} %fusion.97, f32[768,768]{1,0:T(8,128)} %fusion.28, f32[2,768]{1,0:T(2,128)S(1)} %get-tuple-element.302, f32[768,2,128]{0,2,1:T(8,128)S(1)} %fusion.87, ...), kind=kOutput, calls=%fused_computation.66 | convolution fusion | flops 1818230784 | bytes 7096320 | tf_op jit(solution)/shard_map/jvp(hts,shp->thp)/dot_general | solution.py:56
  189.7 6.0 %multiply_reduce_fusion.3 = (f32[768]{0:T(1024)S(1)}, f32[768]{0:T(1024)S(1)}, f32[768,256]{0,1:T(8,128)}) fusion(f32[768,2,128]{0,2,1:T(8,128)S(1)} %fusion.56, f32[768,256]{0,1:T(8,128)S(1)} %copy-done.12, f32[256]{0:T(256)S(1)} %copy-done.45, bf16[768,4096]{1,0:T(8,128)(2,1)} %all-gather.6.cloned.1.call-done, bf16[2,4096,256]{2,1,0:T(8,128)(2,1)S(1)} %copy-done.9), kind=kOutput, calls=%fused_computation.93 | convolution fusion | flops 1612970496 | bytes 10755072 | tf_op jit(solution)/shard_map/dot_general | solution.py:114
  195.8 14.1 %all-reduce.10 = (f32[768]{0:T(1024)S(1)}, f32[768]{0:T(1024)S(1)}) all-reduce(f32[768]{0:T(1024)S(1)} %get-tuple-element.274, f32[768]{0:T(1024)S(1)} %get-tuple-element.273), channel_id=1, replica_groups=mesh['ctx'=4,'tp'=8] {'tp'}, use_global_device_ids=true, to_apply=%region_8.9 | all-reduce | flops 1536 | bytes 12288 | tf_op jit(solution)/shard_map/psum | solution.py:151
  217.3 9.8 %all-gather.2 = f32[8,128,128]{2,1,0:T(8,128)} all-gather(f32[2,128,128]{2,1,0:T(8,128)S(1)} %fusion.77), channel_id=4, replica_groups=mesh['ctx'=4,'tp'=8] {'ctx'}, dimensions={0}, use_global_device_ids=true | all-gather | bytes 655360 | tf_op jit(solution)/shard_map/all_gather | solution.py:25
  227.1 6.7 %while.31 = (s32[]{:T(128)}, f32[2,128,128]{2,1,0:T(8,128)S(1)}, s32[]{:T(128)}, f32[4,2,128,128]{3,2,1,0:T(8,128)}, f32[4,2]{1,0:T(4,128)}, /*index=5*/s32[]{:T(128)}, s32[]{:T(128)}, s32[]{:T(128)}, s32[]{:T(128)}) while((s32[]{:T(128)}, f32[2,128,128]{2,1,0:T(8,128)S(1)}, s32[]{:T(128)}, f32[4,2,128,128]{3,2,1,0:T(8,128)}, ...), condition=%wide.region_11.12_spmd.clone, body=%wide.region_10.11_spmd.clone.sunk | while | flops 131080 | bytes 393415 | solution.py:38
  239.8 11.9 %fusion.14 = (f32[768,768]{1,0:T(8,128)}, f32[2,768]{1,0:T(2,128)}, f32[2,768,768]{2,1,0:T(8,128)}) fusion(f32[2,768]{1,0:T(2,128)S(1)} %copy-done.44, f32[768,768]{1,0:T(8,128)} %fusion.28, f32[2,768]{1,0:T(2,128)S(1)} %get-tuple-element.302, f32[768,768]{1,0:T(8,128)} %fusion.97, f32[2,128,768]{2,1,0:T(8,128)} %bitcast.199, f32[768,2,128]{0,2,1:T(8,128)S(1)} %bitcast.196), kind=kOutput, calls=%fused_computation.20 | convolution fusion | flops 1831401984 | bytes 13387776 | tf_op jit(solution)/shard_map/transpose(jvp(hts,shp->thp))/dot_general | solution.py:56
  251.8 4.8 %fusion.53 = f32[768,2,128]{0,2,1:T(8,128)} fusion(f32[2,128,768]{2,1,0:T(8,128)S(1)} %bitcast.200, f32[2,768]{1,0:T(2,128)S(1)} %copy-done.44, f32[768,768]{1,0:T(8,128)S(1)} %copy-done.18, f32[768,768]{1,0:T(8,128)S(1)} %copy-done.17, f32[2,768]{1,0:T(2,128)S(1)} %get-tuple-element.302, f32[768,2,128]{0,2,1:T(8,128)S(1)} %copy-done.21, ...), kind=kOutput, calls=%fused_computation.65 | convolution fusion | flops 1818230784 | bytes 7096320 | tf_op jit(solution)/shard_map/transpose(jvp(hts,shp->thp))/dot_general | solution.py:56
  263.3 3.5 convolution_add_fusion.1
  273.3 3.9 collective-permute-start.1
  277.2 6.4 %fusion.29 = f32[768,4096]{1,0:T(8,128)} fusion(bf16[768,256]{0,1:T(8,128)(2,1)S(1)} %copy-done.20, bf16[2,4096,256]{2,1,0:T(8,128)(2,1)S(1)} %copy-done.10), kind=kOutput, calls=%fused_computation.37 | convolution fusion | flops 1610612736 | bytes 15073280 | tf_op jit(solution)/shard_map/dot_general | solution.py:191
  283.7 6.5 %fusion.116 = f32[768,4096]{1,0:T(8,128)} fusion(bf16[4096,2]{0,1:T(2,128)(2,1)S(1)} %copy-done.25, f32[768,2]{0,1:T(2,128)S(1)} %get-tuple-element.319, f32[1,2,6,128]{3,2,1,0:T(8,128)S(1)} %add_bitcast_fusion, f32[768,2]{0,1:T(2,128)S(1)} %copy-done.23, f32[2,768]{1,0:T(2,128)S(1)} %copy-done.42, f32[2]{0:T(128)S(1)} %copy-done.41, f32[2]{0:T(128)S(1)} %copy-done.39, ...), kind=kOutput, calls=%fused_computation.166 | convolution fusion | flops 12612096 | bytes 12630032 | tf_op jit(solution)/shard_map/dot_general | solution.py:195
  293.4 6.4 %fusion.33 = f32[768,4096]{1,0:T(8,128)} fusion(bf16[2,4096,256]{2,1,0:T(8,128)(2,1)S(1)} %copy-done.10, f32[765,512]{0,1:T(8,128)S(1)} %slice.123, f32[3,512]{0,1:T(8,128)S(1)} %add_add_fusion.1), kind=kOutput, calls=%fused_computation.41 | convolution fusion | flops 1611399168 | bytes 16515072 | tf_op jit(solution)/shard_map/dot_general | solution.py:192
  299.7 23.2 %add_add_fusion = f32[768,4096]{1,0:T(8,128)} fusion(f32[768,4096]{1,0:T(8,128)} %fusion.116, f32[768,4096]{1,0:T(8,128)} %fusion.29, f32[768,4096]{1,0:T(8,128)} %fusion.33, bf16[4096,256]{1,0:T(8,128)(2,1)S(1)} %copy-done, f32[3,512]{0,1:T(8,128)S(1)} %add_add_fusion.1, f32[765,512]{0,1:T(8,128)} %copy-done.2), kind=kOutput, calls=%fused_computation.6 | convolution fusion | flops 9673310208 | bytes 54001664 | tf_op jit(solution)/shard_map/dot_general | solution.py:198
  322.9 126.6 %reduce-scatter.2.cloned.1.call-done = f32[96,4096]{1,0:T(8,128)} async-done(((f32[768,4096]{1,0:T(8,128)}), f32[96,4096]{1,0:T(8,128)}) %reduce-scatter.2.cloned.1.call-update) | async-done | bytes 1572880 | tf_op jit(solution)/shard_map/reduce_scatter | solution.py:201
  (183 shorter events, 61.1 us)
Async XLA Ops:
  6.5 74.0 %copy-start = (bf16[4096,256]{1,0:T(8,128)(2,1)S(1)}, bf16[4096,256]{1,0:T(8,128)(2,1)}, u32[]{:S(2)}) copy-start(bf16[4096,256]{1,0:T(8,128)(2,1)} %param.18) | copy-start | bytes 6291460
  6.5 68.5 %copy-start.24 = (bf16[4096,2]{0,1:T(2,128)(2,1)S(1)}, bf16[4096,2]{0,1:T(2,128)(2,1)}, u32[]{:S(2)}) copy-start(bf16[4096,2]{0,1:T(2,128)(2,1)} %param.19) | copy-start | bytes 49156
  6.5 68.5 %copy-start.47 = (f32[2]{0:T(128)S(1)}, f32[2]{0:T(128)}, u32[]{:S(2)}) copy-start(f32[2]{0:T(128)} %param.22) | copy-start | bytes 28
  6.5 68.5 %all-gather.6.cloned.1.call-start = ((), (), s32[]{:S(2)}) async-start(), calls=%async_computation.1 | async-start | bytes 7077888 | tf_op jit(solution)/shard_map/all_gather | solution.py:109
  7.3 132.8 %all-gather.8.cloned.1.call-start = ((), (), s32[]{:S(2)}) async-start(), calls=%async_computation.2 | async-start | bytes 7077888 | tf_op jit(solution)/shard_map/all_gather | solution.py:110
  8.0 441.6 %reduce-scatter.2.cloned.1.call-start = ((), (), s32[]{:S(2)}) async-start(), calls=%async_computation.3 | async-start | bytes 14155776 | tf_op jit(solution)/shard_map/reduce_scatter | solution.py:201
  8.8 84.4 %copy-start.40 = (f32[2]{0:T(128)}, f32[2]{0:T(128)S(1)}, u32[]{:S(2)}) copy-start(f32[2]{0:T(128)S(1)} %exp.63) | copy-start | bytes 28
  13.8 142.5 %copy-start.30 = (f32[1,512]{1,0:T(1,128)}, f32[1,512]{1,0:T(1,128)S(1)}, u32[]{:S(2)}) copy-start(f32[1,512]{1,0:T(1,128)S(1)} %get-tuple-element.311) | copy-start | bytes 6148
  13.8 142.5 %copy-start.32 = (f32[1,512]{1,0:T(1,128)}, f32[1,512]{1,0:T(1,128)S(1)}, u32[]{:S(2)}) copy-start(f32[1,512]{1,0:T(1,128)S(1)} %get-tuple-element.313) | copy-start | bytes 6148
  13.8 142.5 %copy-start.34 = (f32[1,512]{1,0:T(1,128)}, f32[1,512]{1,0:T(1,128)S(1)}, u32[]{:S(2)}) copy-start(f32[1,512]{1,0:T(1,128)S(1)} %get-tuple-element.314) | copy-start | bytes 6148
  13.8 142.5 %copy-start.36 = (f32[1,512]{1,0:T(1,128)}, f32[1,512]{1,0:T(1,128)S(1)}, u32[]{:S(2)}) copy-start(f32[1,512]{1,0:T(1,128)S(1)} %get-tuple-element.312) | copy-start | bytes 6148
  79.6 101.0 %copy-start.43 = (f32[2,768]{1,0:T(2,128)}, f32[2,768]{1,0:T(2,128)S(1)}, u32[]{:S(2)}) copy-start(f32[2,768]{1,0:T(2,128)S(1)} %get-tuple-element.304) | copy-start | bytes 18436
  89.5 66.3 %collective-permute-start = (bf16[3,512]{0,1:T(8,128)(2,1)S(1)}, bf16[3,512]{0,1:T(8,128)(2,1)S(1)}, u32[]{:S(2)}, u32[]{:S(2)}) collective-permute-start(bf16[3,512]{0,1:T(8,128)(2,1)S(1)} %pad_maximum_fusion.2), channel_id=1, source_target_pairs={{0,8},{8,16},{16,24},{1,9},{9,17},{17,25},{2,10},{10,18},{18,26},{... | collective-permute-start | bytes 9224 | tf_op jit(solution)/shard_map/ppermute | solution.py:20
  93.0 121.2 %copy-start.28 = (f32[768,2]{0,1:T(2,128)}, f32[768,2]{0,1:T(2,128)S(1)}, u32[]{:S(2)}) copy-start(f32[768,2]{0,1:T(2,128)S(1)} %get-tuple-element.301) | copy-start | bytes 18436
  93.2 53.1 %copy-start.38 = (f32[2]{0:T(128)}, f32[2]{0:T(128)S(1)}, u32[]{:S(2)}) copy-start(f32[2]{0:T(128)S(1)} %slice_reduce_fusion.3) | copy-start | bytes 28
  93.4 69.1 %copy-start.26 = (f32[768,2]{0,1:T(2,128)}, f32[768,2]{0,1:T(2,128)S(1)}, u32[]{:S(2)}) copy-start(f32[768,2]{0,1:T(2,128)S(1)} %get-tuple-element.315) | copy-start | bytes 18436
  239.6 17.3 %copy-start.22 = (f32[768,2]{0,1:T(2,128)}, f32[768,2]{0,1:T(2,128)S(1)}, u32[]{:S(2)}) copy-start(f32[768,2]{0,1:T(2,128)S(1)} %get-tuple-element.321) | copy-start | bytes 18436
  239.8 12.0 %copy-start.5 = (f32[768,256]{0,1:T(8,128)S(1)}, f32[768,256]{0,1:T(8,128)}, u32[]{:S(2)}) copy-start(f32[768,256]{0,1:T(8,128)} %copy-done.4) | copy-start | bytes 2359300
  239.8 12.0 %copy-start.17 = (f32[768,768]{1,0:T(8,128)S(1)}, f32[768,768]{1,0:T(8,128)}, u32[]{:S(2)}) copy-start(f32[768,768]{1,0:T(8,128)} %fusion.28) | copy-start | bytes 7077892
  239.8 12.0 %copy-start.18 = (f32[768,768]{1,0:T(8,128)S(1)}, f32[768,768]{1,0:T(8,128)}, u32[]{:S(2)}) copy-start(f32[768,768]{1,0:T(8,128)} %fusion.97) | copy-start | bytes 7077892
  239.8 12.0 %copy-start.21 = (f32[768,2,128]{0,2,1:T(8,128)S(1)}, f32[768,2,128]{0,2,1:T(8,128)}, u32[]{:S(2)}) copy-start(f32[768,2,128]{0,2,1:T(8,128)} %get-tuple-element.322) | copy-start | bytes 2359300
  239.8 12.0 %copy-start.27 = (f32[768,2]{0,1:T(2,128)S(1)}, f32[768,2]{0,1:T(2,128)}, u32[]{:S(2)}) copy-start(f32[768,2]{0,1:T(2,128)} %copy-done.26) | copy-start | bytes 18436
  273.3 10.4 %copy-start.23 = (f32[768,2]{0,1:T(2,128)S(1)}, f32[768,2]{0,1:T(2,128)}, u32[]{:S(2)}) copy-start(f32[768,2]{0,1:T(2,128)} %copy-done.22) | copy-start | bytes 18436
  273.3 18.9 %collective-permute-start.1 = (f32[3,512]{0,1:T(8,128)S(1)}, f32[3,512]{0,1:T(8,128)S(1)}, u32[]{:S(2)}, u32[]{:S(2)}) collective-permute-start(f32[3,512]{0,1:T(8,128)S(1)} %pad_add_fusion.1), channel_id=1, source_target_pairs={{8,0},{16,8},{24,16},{9,1},{17,9},{25,17},{10,2},{18,10},{26,18},{... | collective-permute-start | bytes 18440 | tf_op jit(solution)/shard_map/ppermute | solution.py:20
  (30 other events, 148.5 us)
Sparse Core Ops, SparseCore 0:
  9.0 65.9 all-gather.5
  76.6 63.3 all-gather.7
  323.0 126.4 reduce-scatter.1
where the time goes:
time: 467 us; the launch traced here: 459 us
  waiting for transfers between devices  236 us (51%)
  matrix products  112 us (24%)
  blocking collectives  44.7 us (10%)
  other arithmetic  32.1 us (7%)
  between operations  15 us (3%)
  local copies, waits for them, and re-layouts  11.5 us (2%)
  starting transfers between devices  7.33 us (2%)
    reduce_scatter x1, waiting for transfers between devices, body(): lax.psum_scatter(summed_term, 'tp', scatter_dimension=0, tiled=True)  127 us
    all_gather x1, waiting for transfers between devices, body(): lax.all_gather(normed_rows, 'tp', axis=0, tiled=True)  61.2 us
    all_gather x1, waiting for transfers between devices, body(): lax.all_gather(out_grad, 'tp', axis=0, tiled=True)  46.6 us
    dot_general x3, matrix products, within_shard(): local_part = jnp.einsum('hts,shp->thp', weights, inner_act, precision=EXACT)  25 us
    dot_general x1, matrix products, body(): jnp.dot(d_state, state_float.T, precision=EXACT, preferred_element_type=j...  23.2 us
    all_gather x2, blocking collectives, prefix(): everything = jax.tree.map(lambda part: lax.all_gather(part, axis), value)  21.1 us
    psum x1, blocking collectives, body(): lax.psum((jnp.sum(gated_out * gated_out, axis=1), jnp.sum(norm_gain * out...  14.1 us
    dot_general x3, matrix products, within_shard(): scores = jnp.dot(c_rows, b_rows.T, precision=EXACT)  10.3 us
  transfers between devices with their start and end apart: 5, of which 3 were waited for; matrix products, arithmetic and copies ran while one was open for 9% of the time, Pallas kernels for 0%

commit v1 on v0

v1 whole, which is shorter than its diff:
```python
import math
from functools import partial

import jax
import jax.numpy as jnp
from jax import lax
from jax.experimental import pallas as pl
from jax.experimental.pallas import tpu as pltpu
from jax.sharding import PartitionSpec as P

HEAD_DIM = 128
STATE = 128
CONV = 4
LANES = 128
PAD = 8
EPSILON = 1e-05
EXACT = lax.Precision.HIGHEST
F32 = jnp.float32
BF16 = jnp.bfloat16
PARAMS = dict(compiler_params=pltpu.CompilerParams(vmem_limit_bytes=16 * 1024 * 1024))


def dot(a, b, over=(1, 0), precision=None):
    return lax.dot_general(
        a, b, (((over[0],), (over[1],)), ((), ())), precision=precision, preferred_element_type=F32
    )


def triangle(size, keep):
    rows = lax.broadcasted_iota(jnp.int32, (size, size), 0)
    columns = lax.broadcasted_iota(jnp.int32, (size, size), 1)
    return keep(rows, columns)


def head(h):
    return slice(h * HEAD_DIM, (h + 1) * HEAD_DIM)


def forward_local(
    heads, block, proj, tail, kern, bias, rate,
    act_out, scaled_out, slope_out, step_out, run_out, sig_out, decay_out, table_out, diag_out, states_out,
    own_out, ext,
):
    length = proj.shape[0]
    width = heads * HEAD_DIM
    conv_width = width + 2 * STATE
    ext[0:PAD, :] = tail[...].astype(F32)
    ext[PAD:, :] = proj[:, width : width + conv_width].astype(F32)
    causal = triangle(block, lambda i, j: i >= j)
    lower = causal.astype(F32)
    state = [jnp.zeros((HEAD_DIM, STATE), F32) for _ in range(heads)]
    for k in range(length // block):
        rows = slice(k * block, (k + 1) * block)
        first = k * block + PAD - (CONV - 1)
        value = kern[0:1, :] * ext[first : first + block, :]
        for j in range(1, CONV):
            value = value + kern[j : j + 1, :] * ext[first + j : first + j + block, :]
        sigmoid = 1.0 / (1.0 + jnp.exp(-value))
        act = value * sigmoid
        act_out[rows, :] = act.astype(BF16)
        slope_out[rows, :] = sigmoid * (1.0 + value * (1.0 - sigmoid))
        raw = proj[rows, width + conv_width :].astype(F32) + bias[...]
        grown = jnp.exp(-jnp.abs(raw))
        step = jnp.maximum(raw, 0.0) + jnp.log1p(grown)
        step_out[rows, :] = step
        sig_out[rows, :] = jnp.where(raw >= 0.0, 1.0, grown) / (1.0 + grown)
        run = dot(lower, -step * rate[...], precision=EXACT)
        run_out[rows, :] = run
        run_t = run.T
        b_rows = act[:, width : width + STATE]
        c_rows = act[:, width + STATE :]
        scores = dot(c_rows, b_rows, (1, 1), EXACT)
        for h in range(heads):
            at = k * heads + h
            col = run[:, h : h + 1]
            decay = jnp.where(causal, jnp.exp(jnp.minimum(col - run_t[h : h + 1, :], 0.0)), 0.0)
            table = decay * scores
            scaled = act[:, head(h)] * step[:, h : h + 1]
            scaled_out[rows, head(h)] = scaled.astype(BF16)
            decay_out[rows, head(h)] = decay.astype(BF16)
            table_out[rows, head(h)] = table.astype(BF16)
            diag_out[rows, head(h)] = dot(table, scaled, precision=EXACT)
            states_out[at * HEAD_DIM : (at + 1) * HEAD_DIM, :] = state[h]
            last = run[block - 1 : block, h : h + 1]
            state[h] = jnp.exp(last) * state[h] + dot(
                jnp.exp(last - col) * scaled, b_rows, (0, 0), EXACT
            )
    for h in range(heads):
        own_out[head(h), :] = state[h]


def forward_carried(
    heads, block, proj, act, run, diag, states, weights, *refs,
):
    received = refs[:-6]
    gated_out, silu_out, slope_out, carried_out, states_out, sums_out = refs[-6:]
    length = proj.shape[0]
    width = heads * HEAD_DIM
    entering = []
    for h in range(heads):
        total = jnp.zeros((HEAD_DIM, STATE), F32)
        for i, part in enumerate(received):
            total = total + weights[i * heads + h : i * heads + h + 1, :] * part[head(h), :]
        entering.append(total)
    base = jnp.zeros((1, LANES), F32)
    ones = jnp.ones((8, width), F32)
    for k in range(length // block):
        rows = slice(k * block, (k + 1) * block)
        r = run[rows, :]
        grow = jnp.exp(r)
        reach = jnp.exp(base)
        c_rows = act[rows, width + STATE :].astype(F32)
        for h in range(heads):
            at = k * heads + h
            here = slice(at * HEAD_DIM, (at + 1) * HEAD_DIM)
            state = states[here, :] + reach[:, h : h + 1] * entering[h]
            states_out[here, :] = state.astype(BF16)
            carried = grow[:, h : h + 1] * dot(c_rows, state, (1, 1), EXACT)
            carried_out[rows, head(h)] = carried.astype(BF16)
            out = diag[rows, head(h)] + carried
            gate = proj[rows, head(h)].astype(F32)
            sigmoid = 1.0 / (1.0 + jnp.exp(-gate))
            silu = gate * sigmoid
            silu_out[rows, head(h)] = silu
            gated_out[rows, head(h)] = out * silu
            slope_out[rows, head(h)] = out * sigmoid * (1.0 + gate * (1.0 - sigmoid))
        base = base + r[block - 1 : block, :]
        gated = gated_out[rows, :]
        sums_out[:, rows] = dot(ones, gated * gated, (1, 1), EXACT)


def project_back(grads, weight, gain, gated, sums, local_out, sums_out):
    local = dot(grads[...], weight[...], (1, 1))
    local_out[...] = local
    ones = jnp.ones((8, local.shape[1]), F32)
    cross = dot(ones, gain[...] * local * gated[...], (1, 1), EXACT)
    upper = lax.broadcasted_iota(jnp.int32, cross.shape, 0) < 4
    sums_out[...] = jnp.where(upper, sums[...], cross)


def backward_gate(heads, block, total_width, local, gain, gated, silu, slope, act, run, *refs):
    parts = refs[:-5]
    dgate_out, cot_out, grown_out, blocks_out, own_out = refs[-5:]
    length = local.shape[0]
    width = heads * HEAD_DIM
    pick = lax.broadcasted_iota(jnp.int32, (8, LANES), 0)
    own = [jnp.zeros((HEAD_DIM, STATE), F32) for _ in range(heads)]
    base = jnp.zeros((1, LANES), F32)
    for k in range(length // block):
        rows = slice(k * block, (k + 1) * block)
        sums = parts[0][:, rows]
        for part in parts[1:]:
            sums = sums + part[:, rows]
        square = dot(sums, (pick == 0).astype(F32), (0, 0), EXACT) / total_width
        cross = dot(sums, (pick == 4).astype(F32), (0, 0), EXACT) / total_width
        inverse = lax.rsqrt(square + EPSILON)
        cross = cross * (inverse * inverse * inverse)
        r = run[rows, :]
        grow = jnp.exp(r)
        reach = jnp.exp(base)
        c_rows = act[rows, width + STATE :]
        for h in range(heads):
            at = k * heads + h
            d_gated = inverse * (gain[:, head(h)] * local[rows, head(h)]) - gated[rows, head(h)] * cross
            dgate_out[rows, head(h)] = (d_gated * slope[rows, head(h)]).astype(BF16)
            cot = d_gated * silu[rows, head(h)]
            cot_out[rows, head(h)] = cot.astype(BF16)
            grown = (grow[:, h : h + 1] * cot).astype(BF16)
            grown_out[rows, head(h)] = grown
            entering = dot(grown, c_rows, (0, 0))
            blocks_out[at * HEAD_DIM : (at + 1) * HEAD_DIM, :] = entering
            own[h] = own[h] + reach[:, h : h + 1] * entering
        base = base + r[block - 1 : block, :]
    for h in range(heads):
        own_out[head(h), :] = own[h]


def backward_local(
    heads, block, cot, grown, act, scaled, decays, table, states, carried, u_out, dbc_out, decay_out
):
    length = cot.shape[0]
    width = heads * HEAD_DIM
    before = triangle(block, lambda i, j: i > j)
    upper = triangle(block, lambda i, j: i <= j).astype(BF16)
    lane = lax.broadcasted_iota(jnp.int32, (block, LANES), 1)
    for k in range(length // block):
        rows = slice(k * block, (k + 1) * block)
        b_rows = act[rows, width : width + STATE]
        c_rows = act[rows, width + STATE :]
        d_brows = jnp.zeros((block, STATE), F32)
        d_crows = jnp.zeros((block, STATE), F32)
        decay = jnp.zeros((block, LANES), F32)
        for h in range(heads):
            at = k * heads + h
            g = cot[rows, head(h)]
            weights = table[rows, head(h)]
            inner = dot(g, scaled[rows, head(h)], (1, 1))
            pairs = (decays[rows, head(h)].astype(F32) * inner).astype(BF16)
            mixed = (weights.astype(F32) * inner).astype(BF16)
            d_crows = d_crows + dot(pairs, b_rows)
            d_crows = d_crows + dot(grown[rows, head(h)], states[at * HEAD_DIM : (at + 1) * HEAD_DIM, :])
            d_brows = d_brows + dot(pairs, c_rows, (0, 0))
            u_out[rows, head(h)] = dot(weights, g, (0, 0))
            through = (g.astype(F32) * carried[rows, head(h)].astype(F32)).astype(BF16)
            spread = jnp.where(before, dot(upper, mixed), 0.0) + dot(upper, through)
            decay = jnp.where(lane == h, jnp.sum(spread, axis=1, keepdims=True), decay)
        dbc_out[rows, :STATE] = d_brows
        dbc_out[rows, STATE:] = d_crows
        decay_out[rows, :] = decay


def backward_carried(
    heads, block, dgate, act, scaled, slope, step, run, sig, rate, kern, states, blocks, u, dbc, decay, weights,
    *refs,
):
    received = refs[:-4]
    cat_out, end_out, tail_out, scr = refs[-4:]
    length = dgate.shape[0]
    width = heads * HEAD_DIM
    conv_width = width + 2 * STATE
    strict = triangle(block, lambda i, j: i > j).astype(BF16)
    lane = lax.broadcasted_iota(jnp.int32, (block, LANES), 1)
    scr[0:PAD, :] = jnp.zeros((PAD, conv_width), F32)
    scr[PAD + length :, :] = jnp.zeros((PAD, conv_width), F32)
    cat_out[:, :width] = dgate[...]
    leaving = []
    for h in range(heads):
        total = jnp.zeros((HEAD_DIM, STATE), F32)
        for i, part in enumerate(received):
            total = total + weights[i * heads + h : i * heads + h + 1, :] * part[head(h), :]
        leaving.append(total)
    for k in reversed(range(length // block)):
        rows = slice(k * block, (k + 1) * block)
        into = slice(PAD + k * block, PAD + (k + 1) * block)
        r = run[rows, :]
        last = r[block - 1 : block, :]
        shrink = jnp.exp(last - r)
        whole = jnp.exp(last)
        b_rows = act[rows, width : width + STATE]
        d_brows = dbc[rows, :STATE]
        d_step = jnp.zeros((block, LANES), F32)
        for h in range(heads):
            at = k * heads + h
            here = slice(at * HEAD_DIM, (at + 1) * HEAD_DIM)
            cot_state = leaving[h].astype(BF16)
            past = shrink[:, h : h + 1] * dot(b_rows, cot_state, (1, 1))
            total = u[rows, head(h)] + past
            moved = scaled[rows, head(h)].astype(F32)
            d_brows = d_brows + dot((shrink[:, h : h + 1] * moved).astype(BF16), cot_state)
            kept = whole[:, h : h + 1] * leaving[h]
            constant = jnp.sum(
                jnp.sum(kept * states[here, :].astype(F32), axis=1, keepdims=True), axis=0, keepdims=True
            )
            spread = dot(strict, (moved * past).astype(BF16))
            d_decay = jnp.sum(spread, axis=1, keepdims=True) + constant + decay[rows, h : h + 1]
            direct = jnp.sum(act[rows, head(h)].astype(F32) * total, axis=1, keepdims=True)
            d_step = jnp.where(lane == h, direct - rate[:, h : h + 1] * d_decay, d_step)
            scr[into, head(h)] = step[rows, h : h + 1] * total * slope[rows, head(h)]
            leaving[h] = kept + blocks[here, :]
        scr[into, width : width + STATE] = d_brows * slope[rows, width : width + STATE]
        scr[into, width + STATE :] = dbc[rows, STATE:] * slope[rows, width + STATE :]
        cat_out[rows, width + conv_width :] = (d_step * sig[rows, :]).astype(BF16)
        value = kern[CONV - 1 : CONV, :] * scr[into, :]
        for j in range(1, CONV):
            value = value + kern[CONV - 1 - j : CONV - j, :] * scr[into.start + j : into.stop + j, :]
        cat_out[rows, width : width + conv_width] = value.astype(BF16)
        if k == length // block - 1:
            end_out[...] = value[block - PAD :, :]
    value = kern[CONV - 1 : CONV, :] * scr[0:PAD, :]
    for j in range(1, CONV):
        value = value + kern[CONV - 1 - j : CONV - j, :] * scr[j : PAD + j, :]
    tail_out[...] = value


def turned(value, axis, by):
    length = lax.axis_size(axis)
    return lax.ppermute(value, axis, [(i, (i + by) % length) for i in range(length)])


def paired(value, by):
    length = lax.axis_size("tp")
    return lax.ppermute(value, "tp", [(i, i ^ by) for i in range(length)])


def shifted(value, axis, by):
    length = lax.axis_size(axis)
    pairs = [(i, i + by) for i in range(length) if 0 <= i + by < length]
    return lax.ppermute(value, axis, pairs)


def shape(*dims, dtype=F32):
    return jax.ShapeDtypeStruct(dims, dtype)


def body(
    normed_rows, out_grad, inner_weight, state_weight, step_weight, conv_inner, conv_state,
    step_bias, decay_log, norm_gain, out_weight,
):
    width = inner_weight.shape[2]
    heads = step_bias.shape[0]
    members = lax.axis_size("tp")
    shards = lax.axis_size("ctx")
    mine = lax.axis_index("ctx")
    length = normed_rows.shape[0] * members
    block = math.gcd(length, 128)
    count = length // block
    conv_width = width + 2 * STATE

    weight_cat = jnp.concatenate(
        [inner_weight[0], inner_weight[1], state_weight, jnp.pad(step_weight, ((0, 0), (0, LANES - heads)))],
        axis=1,
    )
    kern = jnp.concatenate([conv_inner, conv_state], axis=1)
    bias = jnp.pad(step_bias, (0, LANES - heads))[None]
    rate = jnp.pad(jnp.exp(decay_log), (0, LANES - heads))[None]
    gain = norm_gain[None]

    rows_all = lax.all_gather(normed_rows, "tp", axis=0, tiled=True)
    proj = jnp.dot(rows_all, weight_cat, preferred_element_type=F32).astype(BF16)
    grads_all = lax.all_gather(out_grad, "tp", axis=0, tiled=True)

    tail = shifted(proj[length - PAD :, width : width + conv_width], "ctx", 1)
    act, scaled, slope, step, run, sig, decays, table, diag, states, own = pl.pallas_call(
        partial(forward_local, heads, block),
        out_shape=[
            shape(length, conv_width, dtype=BF16),
            shape(length, width, dtype=BF16),
            shape(length, conv_width),
            shape(length, LANES),
            shape(length, LANES),
            shape(length, LANES),
            shape(length, heads * block, dtype=BF16),
            shape(length, heads * block, dtype=BF16),
            shape(length, width),
            shape(count * heads * HEAD_DIM, STATE),
            shape(heads * HEAD_DIM, STATE),
        ],
        scratch_shapes=[pltpu.VMEM((PAD + length, conv_width), F32)],
        name="forward_local",
        **PARAMS,
    )(proj, tail, kern, bias, rate)

    ends = run.reshape(count, block, LANES)[:, block - 1, :heads]
    total_log = jnp.sum(ends, axis=0)
    message = jnp.concatenate([own, jnp.broadcast_to(jnp.pad(total_log, (0, LANES - heads)), (8, LANES))], axis=0)
    received = [turned(message, "ctx", by) for by in range(1, shards)]
    logs = [part[heads * HEAD_DIM, :heads] for part in received]
    entering_weights = []
    between = jnp.zeros((heads,), F32)
    for by in range(1, shards):
        entering_weights.append(jnp.where(mine >= by, jnp.exp(between), 0.0))
        between = between + jnp.where(mine >= by, logs[by - 1], 0.0)
    leaving_weights = []
    between = jnp.zeros((heads,), F32)
    for by in range(1, shards):
        leaving_weights.append(jnp.where(mine + by < shards, jnp.exp(between), 0.0))
        between = between + jnp.where(mine + by < shards, logs[shards - by - 1], 0.0)

    def spread(parts):
        flat = jnp.concatenate(parts)
        return jnp.broadcast_to(flat[:, None], (flat.shape[0], LANES))

    gated, silu, gate_slope, carried, full_states, squares = pl.pallas_call(
        partial(forward_carried, heads, block),
        out_shape=[
            shape(length, width),
            shape(length, width),
            shape(length, width),
            shape(length, width, dtype=BF16),
            shape(count * heads * HEAD_DIM, STATE, dtype=BF16),
            shape(8, length),
        ],
        name="forward_carried",
        **PARAMS,
    )(proj, act, run, diag, states, spread(entering_weights), *received)

    depth = out_grad.shape[1]
    local, sums = pl.pallas_call(
        project_back,
        grid=(count,),
        in_specs=[
            pl.BlockSpec((block, depth), lambda i: (i, 0)),
            pl.BlockSpec((width, depth), lambda i: (0, 0)),
            pl.BlockSpec((1, width), lambda i: (0, 0)),
            pl.BlockSpec((block, width), lambda i: (i, 0)),
            pl.BlockSpec((8, block), lambda i: (0, i)),
        ],
        out_specs=[
            pl.BlockSpec((block, width), lambda i: (i, 0)),
            pl.BlockSpec((8, block), lambda i: (0, i)),
        ],
        out_shape=[shape(length, width), shape(8, length)],
        name="project_back",
        **PARAMS,
    )(grads_all, out_weight, gain, gated, squares)

    sums = sums + paired(sums, 1)
    parts = [sums] + [turned(sums, "tp", by) for by in range(2, members, 2)]

    dgate, cot, grown, blocks, own_cot = pl.pallas_call(
        partial(backward_gate, heads, block, width * members),
        out_shape=[
            shape(length, width, dtype=BF16),
            shape(length, width, dtype=BF16),
            shape(length, width, dtype=BF16),
            shape(count * heads * HEAD_DIM, STATE),
            shape(heads * HEAD_DIM, STATE),
        ],
        name="backward_gate",
        **PARAMS,
    )(local, gain, gated, silu, gate_slope, act, run, *parts)

    returned = [turned(own_cot, "ctx", -by) for by in range(1, shards)]

    u, dbc, decay = pl.pallas_call(
        partial(backward_local, heads, block),
        out_shape=[shape(length, width), shape(length, 2 * STATE), shape(length, LANES)],
        name="backward_local",
        **PARAMS,
    )(cot, grown, act, scaled, decays, table, full_states, carried)

    cat, end, tail_cot = pl.pallas_call(
        partial(backward_carried, heads, block),
        out_shape=[
            shape(length, width + conv_width + LANES, dtype=BF16),
            shape(PAD, conv_width),
            shape(PAD, conv_width),
        ],
        scratch_shapes=[pltpu.VMEM((length + 2 * PAD, conv_width), F32)],
        name="backward_carried",
        **PARAMS,
    )(
        dgate, act, scaled, slope, step, run, sig, rate, kern, full_states, blocks, u, dbc, decay,
        spread(leaving_weights), *returned,
    )

    incoming = shifted(tail_cot, "ctx", -1)
    cat = lax.dynamic_update_slice(cat, (end + incoming).astype(BF16), (length - PAD, width))
    summed = dot(cat, weight_cat, (1, 1)).astype(BF16)
    return lax.psum_scatter(summed, "tp", scatter_dimension=0, tiled=True)


def solution(mesh):
    placed = (
        P(("ctx", "tp"), None),
        P(("ctx", "tp"), None),
        P(None, None, "tp"),
        P(),
        P(None, "tp"),
        P(None, "tp"),
        P(),
        P("tp"),
        P("tp"),
        P("tp"),
        P("tp", None),
    )
    return jax.shard_map(
        body, mesh=mesh, in_specs=placed, out_specs=P(("ctx", "tp"), None), check_vma=False
    )
```

time: 467 us -> 280 us (0.60); the launches traced: 459 us -> 277 us
  matrix products: 112 us -> 20.5 us
  waiting for transfers between devices: 236 us -> 160 us
  blocking collectives: 44.7 us -> 0 us
  other arithmetic: 32.1 us -> 0.21 us
  local copies, waits for them, and re-layouts: 11.5 us -> 40.7 us
  Pallas kernels: 0 us -> 24.7 us
  starting transfers between devices: 7.33 us -> 17.6 us
    dot_general x21 -> x2, matrix products: 112 us -> 20.5 us  [the longest x1 11.2 us: body(): jnp.dot(rows_all, weight_cat, preferred_element_type=F32).astype(BF16)]
    reduce_scatter x1, waiting for transfers between devices: 127 us -> 71 us  [body(): return lax.psum_scatter(summed, 'tp', scatter_dimension=0, tiled=True)]
    all_gather x2, waiting for transfers between devices: 108 us -> 74.2 us  [the longest x1 59.1 us: body(): rows_all = lax.all_gather(normed_rows, 'tp', axis=0, tiled=True)]
    unnamed x102 -> x92, local copies, waits for them, and re-layouts: 5.95 us -> 34.7 us
    pallas_call x0 -> x6, Pallas kernels: none -> 24.7 us  [the longest x1 6.81 us: body(): pl.pallas_call(project_back, grid=(count,), in_specs=[pl.BlockSpec((block...]
    all_gather x2 -> x0, blocking collectives: 21.1 us -> none  [prefix(): everything = jax.tree.map(lambda part: lax.all_gather(part, axis), value)]
    psum x1 -> x0, blocking collectives: 14.1 us -> none  [body(): lax.psum((jnp.sum(gated_out * gated_out, axis=1), jnp.sum(norm_gain * out...]
    ppermute x0 -> x10, starting transfers between devices: none -> 10.7 us  [the longest x9 10.5 us: turned(): lax.ppermute(value, axis, [(i, (i + by) % length) for i in range(length)])]
  transfers between devices with their start and end apart: 5 -> 15, of which waited for: 3 -> 10; matrix products, arithmetic and copies ran while one was open for 9% -> 7% of each run, Pallas kernels for 0% -> 4%
where the time goes in v1:
time: 280 us; the launch traced here: 277 us
  waiting for transfers between devices  160 us (57%)
  local copies, waits for them, and re-layouts  40.7 us (15%)
  Pallas kernels  24.7 us (9%)
  matrix products  20.5 us (7%)
  starting transfers between devices  17.6 us (6%)
  between operations  13.3 us (5%)
    reduce_scatter x1, waiting for transfers between devices, body(): return lax.psum_scatter(summed, 'tp', scatter_dimension=0, tiled=True)  71 us
    all_gather x1, waiting for transfers between devices, body(): rows_all = lax.all_gather(normed_rows, 'tp', axis=0, tiled=True)  59.1 us
    unnamed x92, local copies, waits for them, and re-layouts  34.7 us
    all_gather x1, waiting for transfers between devices, body(): grads_all = lax.all_gather(out_grad, 'tp', axis=0, tiled=True)  15.1 us
    dot_general x1, matrix products, body(): jnp.dot(rows_all, weight_cat, preferred_element_type=F32).astype(BF16)  11.2 us
    ppermute x9, starting transfers between devices, turned(): lax.ppermute(value, axis, [(i, (i + by) % length) for i in range(length)])  10.5 us
    dot_general x1, matrix products, dot(): lax.dot_general(a, b, (((over[0],), (over[1],)), ((), ())), precision=pre...  9.25 us
    ppermute x9, waiting for transfers between devices, turned(): lax.ppermute(value, axis, [(i, (i + by) % length) for i in range(length)])  7.45 us
  transfers between devices with their start and end apart: 15, of which 10 were waited for; matrix products, arithmetic and copies ran while one was open for 7% of the time, Pallas kernels for 4%

profile of v1, /device:TPU:4, one launch (start us, length us, event | category | flops | bytes accessed | tf_op | source)
XLA Modules:
  0.0 277.3 jit_solution(12527827687471898691)
XLA Ops:
  11.4 4.4 %slice_bitcast_fusion.1 = (bf16[4096,256]{1,0:T(8,128)(2,1)}, bf16[4096,256]{1,0:T(8,128)(2,1)}) fusion(bf16[2,4096,256]{2,1,0:T(8,128)(2,1)} %param.13), kind=kLoop, calls=%fused_computation.5 | loop fusion | bytes 8388608 | tf_op jit(solution)/shard_map/squeeze | solution.py:310
  15.9 59.1 %all-gather.5.cloned.1.call-done = bf16[768,4096]{1,0:T(8,128)(2,1)} async-done(((bf16[96,4096]{1,0:T(8,128)(2,1)}), bf16[768,4096]{1,0:T(8,128)(2,1)}) %all-gather.5.cloned.1.call-update) | async-done | bytes 6291472 | tf_op jit(solution)/shard_map/all_gather | solution.py:318
  75.0 11.2 %fusion.2.proj = bf16[768,896]{1,0:T(8,128)(2,1)S(1)} fusion(bf16[768,4096]{1,0:T(8,128)(2,1)} %all-gather.5.cloned.1.call-done, bf16[4096,2]{1,0:T(8,128)(2,1)S(1)} %copy.13, bf16[4096,256]{1,0:T(8,128)(2,1)} %param.14, bf16[4096,256]{1,0:T(8,128)(2,1)} %get-tuple-element.66, bf16[4096,256]{1,0:T(8,128)(2,1)} %get-tuple-element.65), kind=kOutput, calls=%fused_computation.7 | convolution fusion | flops 5674532864 | bytes 13975552 | tf_op jit(solution)/shard_map/dot_general | solution.py:319
  86.3 3.4 %collective-permute-start = (bf16[8,512]{1,0:T(8,128)(2,1)S(1)}, bf16[8,512]{1,0:T(8,128)(2,1)S(1)}, u32[]{:S(2)}, u32[]{:S(2)}) collective-permute-start(bf16[8,512]{1,0:T(8,128)(2,1)S(1)} %slice.28), channel_id=1, source_target_pairs={{0,8},{8,16},{16,24},{1,9},{9,17},{17,25},{2,10},{10,18},{18,26},{... | collective-permute-start | bytes 24584 | tf_op jit(solution)/shard_map/ppermute | solution.py:288
  89.7 3.0 %collective-permute-done.tail = bf16[8,512]{1,0:T(8,128)(2,1)S(1)} collective-permute-done((bf16[8,512]{1,0:T(8,128)(2,1)S(1)}, bf16[8,512]{1,0:T(8,128)(2,1)S(1)}, u32[]{:S(2)}, u32[]{:S(2)}) %collective-permute-start) | collective-permute-done | bytes 8224 | tf_op jit(solution)/shard_map/ppermute | solution.py:288
  92.7 4.8 %forward_local.1 = (bf16[768,512]{1,0:T(8,128)(2,1)S(1)}, bf16[768,256]{1,0:T(8,128)(2,1)S(1)}, f32[768,512]{1,0:T(8,128)S(1)}, f32[768,128]{1,0:T(8,128)S(1)}, ...) custom-call(bf16[768,896]{1,0:T(8,128)(2,1)S(1)} %fusion.2.proj, ...), custom_call_target="tpu_custom_call" | custom-call | tf_op jit(solution)/shard_map/forward_local/pallas_call | solution.py:323
  105.6 1.8 collective-permute-start.3
  107.4 4.5 %collective-permute-done.1.refs_0_ = f32[264,128]{1,0:T(8,128)S(1)} collective-permute-done((f32[264,128]{1,0:T(8,128)S(1)}, f32[264,128]{1,0:T(8,128)S(1)}, u32[]{:S(2)}, u32[]{:S(2)}) %collective-permute-start.1) | collective-permute-done | bytes 135200 | tf_op jit(solution)/shard_map/ppermute | solution.py:277
  118.2 3.5 %forward_carried.1 = (f32[768,256]{1,0:T(8,128)S(1)}, f32[768,256]{1,0:T(8,128)S(1)}, f32[768,256]{1,0:T(8,128)S(1)}, bf16[768,256]{1,0:T(8,128)(2,1)S(1)}, bf16...) custom-call(bf16[768,896]{1,0:T(8,128)(2,1)S(1)} %fusion.2.proj, bf16[768,512]{1,0:T(8,128)(2,1)S(1)} %get-tuple-element.35.act, ...), custom_call_target="tpu_custom_call" | custom-call | tf_op jit(solution)/shard_map/forward_carried/pallas_call | solution.py:363
  125.0 15.1 %all-gather.3.cloned.1.call-done.grads = bf16[768,4096]{1,0:T(8,128)(2,1)} async-done(((bf16[96,4096]{1,0:T(8,128)(2,1)}), bf16[768,4096]{1,0:T(8,128)(2,1)}) %all-gather.3.cloned.1.call-update) | async-done | bytes 6291472 | tf_op jit(solution)/shard_map/all_gather | solution.py:320
  140.1 2.8 %copy-done = bf16[768,4096]{1,0:T(8,128)(2,1)S(1)} copy-done((bf16[768,4096]{1,0:T(8,128)(2,1)S(1)}, bf16[768,4096]{1,0:T(8,128)(2,1)}, u32[]{:S(2)}) %copy-start) | copy-done | bytes 6291480
  142.9 1.6 copy-done.1
  144.5 6.8 %project_back.1 = (f32[768,256]{1,0:T(8,128)S(1)}, f32[8,768]{1,0:T(8,128)S(1)}) custom-call(bf16[768,4096]{1,0:T(8,128)(2,1)S(1)} %copy-done, bf16[256,4096]{1,0:T(8,128)(2,1)S(1)} %copy-done.1, f32[1,256]{1,0:T(1,128)S(1)} %bitcast.23, f32[768,256]{1,0:T(8,128)S(1)} %get-tuple-element.40.gated, f32[8,768]{1,0:T(8,128)S(1)} %get-tuple-element.41.sums), custom_call_target="tpu_custom_call" | custom-call | tf_op jit(solution)/shard_map/project_back/pallas_call | solution.py:378
  152.5 1.5 collective-permute-start.6
  154.0 2.5 collective-permute-start.7
  156.5 1.7 collective-permute-done.5.refs_1_
  158.7 3.2 %backward_gate.1 = (bf16[768,256]{1,0:T(8,128)(2,1)S(1)}, bf16[768,256]{1,0:T(8,128)(2,1)S(1)}, bf16[768,256]{1,0:T(8,128)(2,1)S(1)}, f32[1536,128]{1,0:T(8,128)S(1)}, f32[256,128]{1,0:T(8,128)}) custom-call(f32[768,256]{1,0:T(8,128)S(1)} %get-tuple-element.42.local, f32[1,256]{1,0:T(1,128)S(1)} %bitcast.24, f32[768,256]{1,0:T(8,128)S(1)} %get-tuple-element.40.gated, ...), custom_call_target="tpu_custom_call" | custom-call | tf_op jit(solution)/shard_map/backward_gate/pallas_call | solution.py:400
  165.1 1.5 collective-permute-start.10
  173.7 2.8 %backward_local.1 = (f32[768,256]{1,0:T(8,128)S(1)}, f32[768,256]{1,0:T(8,128)S(1)}, f32[768,128]{1,0:T(8,128)S(1)}) custom-call(bf16[768,256]{1,0:T(8,128)(2,1)S(1)} %copy-done.31, bf16[768,256]{1,0:T(8,128)(2,1)S(1)} %copy-done.33, bf16[768,512]{1,0:T(8,128)(2,1)S(1)} %get-tuple-element.35.act, bf16[768,256]{1,0:T(8,128)(2,1)S(1)} %copy-done.3, ...), custom_call_target="tpu_custom_call" | custom-call | tf_op jit(solution)/shard_map/backward_local/pallas_call | solution.py:415
  181.2 3.6 %backward_carried.1 = (bf16[768,896]{1,0:T(8,128)(2,1)S(1)}, f32[8,512]{1,0:T(8,128)S(1)}, f32[8,512]{1,0:T(8,128)S(1)}) custom-call(bf16[768,256]{1,0:T(8,128)(2,1)S(1)} %copy-done.23, bf16[768,512]{1,0:T(8,128)(2,1)S(1)} %get-tuple-element.35.act, bf16[768,256]{1,0:T(8,128)(2,1)S(1)} %copy-done.3, f32[768,512]{1,0:T(8,128)S(1)} %copy-done.7, ...), custom_call_target="tpu_custom_call" | custom-call | tf_op jit(solution)/shard_map/backward_carried/pallas_call | solution.py:422
  184.8 3.4 %collective-permute-start.11 = (f32[8,512]{1,0:T(8,128)S(1)}, f32[8,512]{1,0:T(8,128)S(1)}, u32[]{:S(2)}, u32[]{:S(2)}) collective-permute-start(f32[8,512]{1,0:T(8,128)S(1)} %get-tuple-element.64), channel_id=1, source_target_pairs={{8,0},{16,8},{24,16},{9,1},{17,9},{25,17},{10,2},{18,10},{26,18},{... | collective-permute-start | bytes 49160 | tf_op jit(solution)/shard_map/ppermute | solution.py:288
  188.2 2.2 collective-permute-done.11
  190.5 9.3 %convolution_convert_fusion = bf16[768,4096]{1,0:T(8,128)(2,1)} fusion(bf16[768,896]{1,0:T(8,128)(2,1)S(1)} %fusion.3, bf16[4096,2]{1,0:T(8,128)(2,1)S(1)} %copy-done.42, bf16[4096,256]{1,0:T(8,128)(2,1)S(1)} %copy-done.44, bf16[4096,256]{1,0:T(8,128)(2,1)S(1)} %copy-done.40, bf16[4096,256]{1,0:T(8,128)(2,1)S(1)} %copy-done.39), kind=kOutput, calls=%fused_computation.3 | convolution fusion | flops 5676990464 | bytes 13975552 | tf_op jit(solution)/shard_map/dot_general | solution.py:24
  199.7 71.0 %reduce-scatter.2.cloned.1.call-done = bf16[96,4096]{1,0:T(8,128)(2,1)} async-done(((bf16[768,4096]{1,0:T(8,128)(2,1)}), bf16[96,4096]{1,0:T(8,128)(2,1)}) %reduce-scatter.2.cloned.1.call-update) | async-done | bytes 786448 | tf_op jit(solution)/shard_map/reduce_scatter | solution.py:440
  (127 shorter events, 39.3 us)
Async XLA Ops:
  6.5 68.5 %all-gather.5.cloned.1.call-start = ((), (), s32[]{:S(2)}) async-start(), calls=%async_computation.2 | async-start | bytes 7077888 | tf_op jit(solution)/shard_map/all_gather | solution.py:318
  7.3 132.8 %all-gather.3.cloned.1.call-start = ((), (), s32[]{:S(2)}) async-start(), calls=%async_computation.1 | async-start | bytes 7077888 | tf_op jit(solution)/shard_map/all_gather | solution.py:320
  8.0 262.7 %reduce-scatter.2.cloned.1.call-start = ((), (), s32[]{:S(2)}) async-start(), calls=%async_computation.3 | async-start | bytes 7077888 | tf_op jit(solution)/shard_map/reduce_scatter | solution.py:440
  9.4 76.9 %copy-start.41 = (bf16[4096,2]{1,0:T(8,128)(2,1)}, bf16[4096,2]{1,0:T(8,128)(2,1)S(1)}, u32[]{:S(2)}) copy-start(bf16[4096,2]{1,0:T(8,128)(2,1)S(1)} %copy.13) | copy-start | bytes 49156
  75.0 14.7 %copy-start.43 = (f32[2]{0:T(128)S(1)}, f32[2]{0:T(128)}, u32[]{:S(2)}) copy-start(f32[2]{0:T(128)} %param.18) | copy-start | bytes 28
  86.3 53.8 %copy-start.38 = (f32[256]{0:T(256)S(1)}, f32[256]{0:T(256)}, u32[]{:S(2)}) copy-start(f32[256]{0:T(256)} %param.20) | copy-start | bytes 3076
  86.3 6.4 %collective-permute-start = (bf16[8,512]{1,0:T(8,128)(2,1)S(1)}, bf16[8,512]{1,0:T(8,128)(2,1)S(1)}, u32[]{:S(2)}, u32[]{:S(2)}) collective-permute-start(bf16[8,512]{1,0:T(8,128)(2,1)S(1)} %slice.28), channel_id=1, source_target_pairs={{0,8},{8,16},{16,24},{1,9},{9,17},{17,25},{2,10},{10,18},{18,26},{... | collective-permute-start | bytes 24584 | tf_op jit(solution)/shard_map/ppermute | solution.py:288
  104.4 7.4 %collective-permute-start.1 = (f32[264,128]{1,0:T(8,128)S(1)}, f32[264,128]{1,0:T(8,128)S(1)}, u32[]{:S(2)}, u32[]{:S(2)}) collective-permute-start(f32[264,128]{1,0:T(8,128)S(1)} %pad_maximum_fusion), channel_id=1, source_target_pairs={{0,8},{8,16},{16,24},{24,0},{1,9},{9,17},{17,25},{25,1},{2,10},{10... | collective-permute-start | bytes 405512 | tf_op jit(solution)/shard_map/ppermute | solution.py:277
  105.0 7.6 %collective-permute-start.2 = (f32[264,128]{1,0:T(8,128)S(1)}, f32[264,128]{1,0:T(8,128)S(1)}, u32[]{:S(2)}, u32[]{:S(2)}) collective-permute-start(f32[264,128]{1,0:T(8,128)S(1)} %pad_maximum_fusion), channel_id=1, source_target_pairs={{0,16},{8,24},{16,0},{24,8},{1,17},{9,25},{17,1},{25,9},{2,18},{10... | collective-permute-start | bytes 405512 | tf_op jit(solution)/shard_map/ppermute | solution.py:277
  105.6 7.1 %collective-permute-start.3 = (f32[264,128]{1,0:T(8,128)S(1)}, f32[264,128]{1,0:T(8,128)S(1)}, u32[]{:S(2)}, u32[]{:S(2)}) collective-permute-start(f32[264,128]{1,0:T(8,128)S(1)} %pad_maximum_fusion), channel_id=1, source_target_pairs={{0,24},{8,0},{16,8},{24,16},{1,25},{9,1},{17,9},{25,17},{2,26},{10... | collective-permute-start | bytes 405512 | tf_op jit(solution)/shard_map/ppermute | solution.py:277
  144.5 14.2 %copy-start.13 = (f32[768,256]{1,0:T(8,128)S(1)}, f32[768,256]{1,0:T(8,128)}, u32[]{:S(2)}) copy-start(f32[768,256]{1,0:T(8,128)} %copy-done.12) | copy-start | bytes 2359300
  144.5 24.2 %copy-start.3 = (bf16[768,256]{1,0:T(8,128)(2,1)S(1)}, bf16[768,256]{1,0:T(8,128)(2,1)}, u32[]{:S(2)}) copy-start(bf16[768,256]{1,0:T(8,128)(2,1)} %copy-done.2) | copy-start | bytes 1179652
  144.5 24.2 %copy-start.5 = (bf16[1536,128]{1,0:T(8,128)(2,1)S(1)}, bf16[1536,128]{1,0:T(8,128)(2,1)}, u32[]{:S(2)}) copy-start(bf16[1536,128]{1,0:T(8,128)(2,1)} %copy-done.4) | copy-start | bytes 1179652
  151.3 25.3 %copy-start.19 = (f32[768,128]{1,0:T(8,128)S(1)}, f32[768,128]{1,0:T(8,128)}, u32[]{:S(2)}) copy-start(f32[768,128]{1,0:T(8,128)} %copy-done.18) | copy-start | bytes 1179652
  151.3 1.2 collective-permute-start.4
  152.5 5.7 %collective-permute-start.5 = (f32[8,768]{1,0:T(8,128)S(1)}, f32[8,768]{1,0:T(8,128)S(1)}, u32[]{:S(2)}, u32[]{:S(2)}) collective-permute-start(f32[8,768]{1,0:T(8,128)S(1)} %add.36.refs_0_), channel_id=1, source_target_pairs={{0,2},{1,3},{2,4},{3,5},{4,6},{5,7},{6,0},{7,1},{8,10},{9,11},{10,... | collective-permute-start | bytes 73736 | tf_op jit(solution)/shard_map/ppermute | solution.py:277
  152.5 5.7 %collective-permute-start.6 = (f32[8,768]{1,0:T(8,128)S(1)}, f32[8,768]{1,0:T(8,128)S(1)}, u32[]{:S(2)}, u32[]{:S(2)}) collective-permute-start(f32[8,768]{1,0:T(8,128)S(1)} %add.36.refs_0_), channel_id=1, source_target_pairs={{0,4},{1,5},{2,6},{3,7},{4,0},{5,1},{6,2},{7,3},{8,12},{9,13},{10,... | collective-permute-start | bytes 73736 | tf_op jit(solution)/shard_map/ppermute | solution.py:277
  154.0 4.7 %collective-permute-start.7 = (f32[8,768]{1,0:T(8,128)S(1)}, f32[8,768]{1,0:T(8,128)S(1)}, u32[]{:S(2)}, u32[]{:S(2)}) collective-permute-start(f32[8,768]{1,0:T(8,128)S(1)} %add.36.refs_0_), channel_id=1, source_target_pairs={{0,6},{1,7},{2,0},{3,1},{4,2},{5,3},{6,4},{7,5},{8,14},{9,15},{10,... | collective-permute-start | bytes 73736 | tf_op jit(solution)/shard_map/ppermute | solution.py:277
  165.1 11.4 %collective-permute-start.10 = (f32[256,128]{1,0:T(8,128)}, f32[256,128]{1,0:T(8,128)S(1)}, u32[]{:S(2)}, u32[]{:S(2)}) collective-permute-start(f32[256,128]{1,0:T(8,128)} %get-tuple-element.61), channel_id=1, source_target_pairs={{0,8},{8,16},{16,24},{24,0},{1,9},{9,17},{17,25},{25,1},{2,10},{10... | collective-permute-start | bytes 393224 | tf_op jit(solution)/shard_map/ppermute | solution.py:277
  166.6 10.0 %collective-permute-start.8 = (f32[256,128]{1,0:T(8,128)}, f32[256,128]{1,0:T(8,128)S(1)}, u32[]{:S(2)}, u32[]{:S(2)}) collective-permute-start(f32[256,128]{1,0:T(8,128)} %get-tuple-element.61), channel_id=1, source_target_pairs={{0,24},{8,0},{16,8},{24,16},{1,25},{9,1},{17,9},{25,17},{2,26},{10... | collective-permute-start | bytes 393224 | tf_op jit(solution)/shard_map/ppermute | solution.py:277
  168.0 8.5 %collective-permute-start.9 = (f32[256,128]{1,0:T(8,128)}, f32[256,128]{1,0:T(8,128)S(1)}, u32[]{:S(2)}, u32[]{:S(2)}) collective-permute-start(f32[256,128]{1,0:T(8,128)} %get-tuple-element.61), channel_id=1, source_target_pairs={{0,16},{8,24},{16,0},{24,8},{1,17},{9,25},{17,1},{25,9},{2,18},{10... | collective-permute-start | bytes 393224 | tf_op jit(solution)/shard_map/ppermute | solution.py:277
  173.7 16.8 %copy-start.39 = (bf16[4096,256]{1,0:T(8,128)(2,1)S(1)}, bf16[4096,256]{1,0:T(8,128)(2,1)}, u32[]{:S(2)}) copy-start(bf16[4096,256]{1,0:T(8,128)(2,1)} %get-tuple-element.65) | copy-start | bytes 6291460
  173.7 16.8 %copy-start.42 = (bf16[4096,2]{1,0:T(8,128)(2,1)S(1)}, bf16[4096,2]{1,0:T(8,128)(2,1)}, u32[]{:S(2)}) copy-start(bf16[4096,2]{1,0:T(8,128)(2,1)} %copy-done.41) | copy-start | bytes 49156
  184.8 5.6 %collective-permute-start.11 = (f32[8,512]{1,0:T(8,128)S(1)}, f32[8,512]{1,0:T(8,128)S(1)}, u32[]{:S(2)}, u32[]{:S(2)}) collective-permute-start(f32[8,512]{1,0:T(8,128)S(1)} %get-tuple-element.64), channel_id=1, source_target_pairs={{8,0},{16,8},{24,16},{9,1},{17,9},{25,17},{10,2},{18,10},{26,18},{... | collective-permute-start | bytes 49160 | tf_op jit(solution)/shard_map/ppermute | solution.py:288
  (36 other events, 65.5 us)
Sparse Core Ops, SparseCore 0:
  9.0 65.9 all-gather.4
  76.6 63.3 all-gather.2
  199.9 70.8 reduce-scatter.1
